TPU v7x, 256 devices: a whole 4x4x8 slice. The times are simulated.
256 devices in a mesh: tm: 16 (over z, core), evec: 16 (over y, x).
Axes of the slice: x: 4, y: 4, z: 8, core: 2. Of those that a mesh axis runs over, the one named last changes fastest.
Arguments:
- sink_elemental: bfloat16 [2, 16, 8, 128, 128, 128], P(None, 'tm', None, 'evec'), may hold values from -6 to 6
- source_elemental: bfloat16 [2, 8, 128, 128, 128], P(None, None, None, 'evec', 'tm'), may hold values from -6 to 6
- perambulator: bfloat16 [2, 16, 128, 128], P(None, 'tm'), may hold values from -0.375 to 0.375
- diagram_time: int32 [1024], replicated, may hold values from 0 to 15
- diagram_perm: int32 [1024, 2], replicated, may hold values from 0 to 1
- diagram_ops: int32 [1024, 4], replicated, may hold values from 0 to 7
- diagram_sign: int32 [1024], replicated, may hold values from 0 to 1
Outputs:
- blocks: float32 [2, 16, 2, 8, 8], P(None, 'tm')
- correlator: float32 [2, 16], P(None, 'tm')
All inputs are finite; a program needn't handle non-finite values.
Results may differ from a plain program's by a relative error of at most 0.0003.
Values may be sent and summed in bfloat16 or wider, within the bound.
A program may use at most 128 MiB of HBM per device.

v0:
```python
import functools
import math

import jax
import jax.numpy as jnp
from jax import lax
from jax.experimental import pallas as pl
from jax.experimental.pallas import tpu as pltpu
from jax.sharding import PartitionSpec as P

DIAG_T = 64
NEV = 128
NS = 8
BLOCK = 8
EV = 16
TM = 16
ZS = 8
ROWS = NS * BLOCK
TOP = 32767.0
MESH = pl.DeviceIdType.MESH
F32 = jnp.float32
BF16 = jnp.bfloat16
NT = (((1,), (1,)), ((), ()))
NN = (((1,), (0,)), ((), ()))
FAR_FIRST = (10, 9, 11, 6, 14, 2, 8, 5, 7, 13, 15, 1, 3, 4, 12)


def split_parts(value):
    high = value.astype(BF16)
    return high, (value - high.astype(F32)).astype(BF16)


def iota(shape, axis):
    return lax.broadcasted_iota(jnp.int32, shape, axis)


def kernel(
    sink_ref,
    source_ref,
    peram_ref,
    time_ref,
    perm_ref,
    ops_ref,
    sign_ref,
    blocks_ref,
    corr_ref,
    sink_buf,
    send,
    recv,
    gathered,
    rmat,
    stage,
    tmat,
    total,
    scale_own,
    scale_recv,
    scale_wide,
    left_mat,
    right_mat,
    source_mat,
    counts,
    part_own,
    part_recv,
    sink_sem,
    send_sem,
    recv_sem,
    own_sem,
    scale_sem,
    part_sem,
    ring_sem,
    pair_sem,
    slot_sem,
):
    tm = lax.axis_index("tm")
    ev = lax.axis_index("evec")
    row, column = ev // 4, lax.rem(ev, 4)
    depth, core = tm // 2, lax.rem(tm, 2)

    def peer(step):
        return lax.rem(row + step // 4, 4) * 4 + lax.rem(column + step % 4, 4)

    def slot(step):
        return lax.rem(depth + step + ZS, ZS) * 2 + core

    up, down = (slot(1), ev), (slot(-1), ev)
    pair = (depth * 2 + 1 - core, ev)

    def sink_copy(a):
        return pltpu.make_async_copy(
            sink_ref.at[:, 0, :, a], sink_buf.at[a], sink_sem.at[a]
        )

    for a in range(BLOCK):
        sink_copy(a).start()

    barrier = pltpu.get_barrier_semaphore()
    for step in FAR_FIRST:
        pl.semaphore_signal(barrier, inc=1, device_id=(tm, peer(step)), device_id_type=MESH)
    for device in (up, down, pair):
        pl.semaphore_signal(barrier, inc=1, device_id=device, device_id_type=MESH)

    real, imag = peram_ref[0, 0], peram_ref[1, 0]
    real32, imag32 = real.astype(F32), imag.astype(F32)
    real_t, imag_t = real32.T.astype(BF16), imag32.T.astype(BF16)
    minus, minus_t = (-imag32).astype(BF16), (-imag32.T).astype(BF16)
    left_mat[...] = jnp.concatenate(
        [jnp.concatenate([real_t, minus_t], 1), jnp.concatenate([imag_t, real_t], 1)], 0
    )
    one = jnp.concatenate(
        [jnp.concatenate([real, imag], 1), jnp.concatenate([minus, real], 1)], 0
    )
    right_mat[...] = jnp.concatenate([one, one], 0)
    source_mat[...] = jnp.concatenate(
        [jnp.concatenate([real, minus], 1), jnp.concatenate([imag, real], 1)], 0
    )
    scale_own[...] = jnp.zeros_like(scale_own)

    def transform(a):
        scales = []
        for s2 in range(NS // 2):
            s = 2 * s2
            both = jnp.concatenate(
                [
                    jnp.concatenate([sink_buf[a, 0, s], sink_buf[a, 0, s + 1]], 1),
                    jnp.concatenate([sink_buf[a, 1, s], sink_buf[a, 1, s + 1]], 1),
                ],
                0,
            )
            once = lax.dot_general(left_mat[...], both, NN, preferred_element_type=F32)
            high, low = split_parts(once)
            lines = []
            for h in range(2):
                lanes = slice(h * NEV, (h + 1) * NEV)
                lines.append(
                    jnp.concatenate(
                        [high[:NEV, lanes], high[NEV:, lanes], low[:NEV, lanes], low[NEV:, lanes]], 1
                    )
                )
            twice = lax.dot_general(
                jnp.concatenate(lines, 0), right_mat[...], NN, preferred_element_type=F32
            )
            for h in range(2):
                mine = twice[h * NEV : (h + 1) * NEV]
                top = jnp.maximum(jnp.max(jnp.abs(mine), keepdims=True), 1e-35)
                code = jnp.round(mine * (TOP / top)).astype(jnp.int32)
                packed = (code[:, :NEV] << 16) | (code[:, NEV:] & 0xFFFF)
                send[:, a, pl.ds((s + h) * BLOCK, BLOCK), :] = packed.reshape(EV, BLOCK, NEV)
                scales.append(top * (1.0 / TOP))
        scales = jnp.concatenate(scales, 0)
        scale_own[...] = jnp.where(iota((NS, NEV), 1) == a, scales, scale_own[...])

    def send_copy(a, step):
        there = peer(step)
        return pltpu.make_async_remote_copy(
            send.at[there, a], recv.at[a, ev], send_sem.at[a], recv_sem.at[a],
            device_id=(tm, there), device_id_type=MESH,
        )

    def own_copy(a):
        return pltpu.make_async_copy(send.at[ev, a], recv.at[a, ev], own_sem.at[a])

    def post(a):
        for step in FAR_FIRST:
            send_copy(a, step).start()
        own_copy(a).start()

    def ring_copy(way, step):
        there = (up, down)[way]
        index = slot(-step) if way == 0 else slot(step)
        if step == 0:
            src, dst = source_ref, gathered.at[index]
        elif step < 3:
            src, dst = gathered.at[index], gathered.at[index]
        else:
            src, dst = gathered.at[index, way], gathered.at[index, way]
        return pltpu.make_async_remote_copy(
            src, dst, ring_sem.at[0, way, step], ring_sem.at[1, way, step],
            device_id=there, device_id_type=MESH,
        )

    def ring_arrival(way, step):
        index = slot(-step - 1) if way == 0 else slot(step + 1)
        ref = gathered.at[index] if step < 3 else gathered.at[index, way]
        return pltpu.make_async_copy(ref, ref, ring_sem.at[1, way, step])

    def pair_copy(order):
        step = (0, -1, 1, -2, 2, -3, 3, 4)[order]
        index = slot(step)
        src = source_ref if order == 0 else gathered.at[index]
        return pltpu.make_async_remote_copy(
            src, gathered.at[index], pair_sem.at[0, order], pair_sem.at[1, order],
            device_id=pair, device_id_type=MESH,
        )

    def pair_arrival(order):
        step = (0, -1, 1, -2, 2, -3, 3, 4)[order]
        index = lax.rem(depth + step + ZS, ZS) * 2 + 1 - core
        ref = gathered.at[index]
        return pltpu.make_async_copy(ref, ref, pair_sem.at[1, order])

    sink_copy(0).wait()
    transform(0)
    pl.semaphore_wait(barrier, EV - 1 + 3)
    for way in range(2):
        ring_copy(way, 0).start()
    pair_copy(0).start()
    mine_copy = pltpu.make_async_copy(source_ref, gathered.at[tm], slot_sem)
    mine_copy.start()
    post(0)

    @pl.loop(1, BLOCK)
    def _(a):
        sink_copy(a).wait()
        transform(a)
        post(a)

    def scale_copy(step):
        return pltpu.make_async_remote_copy(
            scale_own, scale_recv.at[ev], scale_sem.at[0], scale_sem.at[1],
            device_id=(tm, peer(step)), device_id_type=MESH,
        )

    for step in FAR_FIRST:
        scale_copy(step).start()

    def place(first):
        nucleon = first // 2
        return (
            perm_ref[nucleon : nucleon + 1, :] * NS + ops_ref[first : first + 1, :]
        ) * NS + ops_ref[first + 1 : first + 2, :]

    phase = jnp.where(time_ref[...] == tm, 1 - 2 * sign_ref[...], 0).astype(F32)
    entries = iota((NEV, phase.shape[1]), 0)
    first_hot = jnp.where(entries == place(0), phase, 0.0).astype(BF16)
    second_hot = jnp.where(entries == place(2), 1.0, 0.0).astype(BF16)
    counts[...] = lax.dot_general(first_hot, second_hot, NT, preferred_element_type=F32)

    for step in range(4):
        for way in range(2):
            ring_arrival(way, step).wait()
        if step < 3:
            for way in range(2):
                ring_copy(way, step + 1).start()
                pair_copy(2 * step + 1 + way).start()
        else:
            pair_copy(7).start()
    mine_copy.wait()
    for order in range(8):
        pair_arrival(order).wait()

    @pl.loop(0, NS)
    def _(u):
        for j2 in range(BLOCK // 2):
            mats = []
            for part in range(2):
                lines = gathered[:, part, u, pl.ds(j2 * 2 * BLOCK, 2 * BLOCK), :].astype(F32)
                mats.append(
                    [
                        lines[:, h * BLOCK : (h + 1) * BLOCK].reshape(NEV, NEV).astype(BF16)
                        for h in range(2)
                    ]
                )
            by_rows = jnp.concatenate(
                [jnp.concatenate([mats[0][h], mats[1][h]], 1) for h in range(2)], 0
            )
            by_lanes = jnp.concatenate(
                [jnp.concatenate([mats[part][0], mats[part][1]], 1) for part in range(2)], 0
            )
            direct = lax.dot_general(source_mat[...], by_rows, NT, preferred_element_type=F32)
            crossed = lax.dot_general(source_mat[...], by_lanes, NN, preferred_element_type=F32)
            for p, result in enumerate((direct, crossed)):
                for h in range(2):
                    at = (p * BLOCK + 2 * j2 + h) * 2 * NEV
                    stage[pl.ds(at, 2 * NEV), :] = result[:, h * NEV : (h + 1) * NEV]

        @pl.loop(0, EV)
        def _(block):
            lanes = pl.ds(pl.multiple_of(block * NEV, NEV), NEV)
            for p in range(2):
                for a in range(BLOCK):
                    tiles = []
                    for part in range(2):
                        at = p * BLOCK * 2 * NEV + part * NEV + a + block * BLOCK
                        value = stage[pl.ds(at, BLOCK, stride=2 * NEV), :]
                        high = value.astype(BF16).astype(F32)
                        tiles += [value, value - high]
                    rows = pl.ds(pl.multiple_of((p * NS + u) * 32, 32), 32)
                    rmat[a, rows, lanes] = jnp.concatenate(tiles, 0).astype(BF16)

    for step in FAR_FIRST[:1]:
        pltpu.make_async_copy(
            scale_recv.at[pl.ds(0, EV - 1)], scale_recv.at[pl.ds(0, EV - 1)], scale_sem.at[1]
        ).wait()
    scale_recv[ev] = scale_own[...]

    @pl.loop(0, EV)
    def _(block):
        tile = scale_recv[block]
        for a in range(BLOCK):
            scale_wide[a, block] = jnp.broadcast_to(tile[:, a : a + 1], (NS, NEV))

    total[...] = jnp.zeros_like(total)

    @pl.loop(0, BLOCK)
    def _(a):
        own_copy(a).wait()
        pltpu.make_async_copy(
            recv.at[a, pl.ds(0, EV - 1)], recv.at[a, pl.ds(0, EV - 1)], recv_sem.at[a]
        ).wait()

        @pl.loop(0, EV)
        def _(block):
            lanes = pl.ds(pl.multiple_of(block * NEV, NEV), NEV)
            scale = jnp.broadcast_to(
                scale_wide[a, block][:, None, :], (NS, BLOCK, NEV)
            ).reshape(ROWS, NEV)
            packed = recv[a, block]
            real_high, real_low = split_parts((packed >> 16).astype(F32) * scale)
            imag_high, imag_low = split_parts(((packed << 16) >> 16).astype(F32) * scale)
            tmat[:, lanes] = jnp.concatenate([real_high, real_low, imag_high, imag_low], 0)

        total[...] += lax.dot_general(rmat[a], tmat[...], NT, preferred_element_type=F32)

    alike = (iota((512, 256), 0) % BLOCK) == (iota((512, 256), 1) % BLOCK)
    kept = jnp.where(alike, total[...], 0.0).reshape(32, 16, 256).sum(axis=1)
    source_row, entry = iota((256, 256), 0), iota((256, 256), 1)
    spread = (source_row // 128 == entry // 128) & (
        (source_row // BLOCK) % NS == (entry % 128) // NS % NS
    )
    lined = lax.dot_general(
        kept, jnp.where(spread, 1.0, 0.0), NN,
        precision=lax.Precision.HIGHEST, preferred_element_type=F32,
    )
    line, entry = iota((32, 128), 0), iota((32, 128), 1)
    wanted = (line // 16 == entry // 64) & (line // 2 % NS == entry % NS)
    real_line = line % 2 == 0
    with_real, with_imag = lined[:, :NEV], lined[:, NEV:]
    real_sum = jnp.where(wanted, jnp.where(real_line, with_real, -with_imag), 0.0)
    imag_sum = jnp.where(wanted, jnp.where(real_line, with_imag, with_real), 0.0)
    part_own[...] = jnp.concatenate(
        [real_sum.sum(axis=0, keepdims=True), imag_sum.sum(axis=0, keepdims=True)], 0
    )

    def part_copy(step):
        return pltpu.make_async_remote_copy(
            part_own, part_recv.at[ev], part_sem.at[0], part_sem.at[1],
            device_id=(tm, peer(step)), device_id_type=MESH,
        )

    for step in FAR_FIRST:
        part_copy(step).start()
    part_recv[ev] = part_own[...]
    pltpu.make_async_copy(
        part_recv.at[pl.ds(0, EV - 1)], part_recv.at[pl.ds(0, EV - 1)], part_sem.at[1]
    ).wait()
    blocks = part_recv[0]
    for block in range(1, EV):
        blocks = blocks + part_recv[block]
    blocks = blocks * NEV ** (-1.5)
    blocks_ref[...] = blocks
    met = lax.dot_general(
        blocks, counts[...], NN, precision=lax.Precision.HIGHEST, preferred_element_type=F32
    )
    real_value = met[0:1] * blocks[0:1] - met[1:2] * blocks[1:2]
    imag_value = met[0:1] * blocks[1:2] + met[1:2] * blocks[0:1]
    value = jnp.concatenate([real_value, imag_value], 0).sum(axis=1, keepdims=True)
    corr_ref[...] = jnp.broadcast_to(value / math.sqrt(DIAG_T), corr_ref.shape)

    @pl.loop(0, BLOCK)
    def _(a):
        pltpu.make_async_copy(
            recv.at[a, pl.ds(0, EV - 1)], recv.at[a, pl.ds(0, EV - 1)], send_sem.at[a]
        ).wait()

    pltpu.make_async_copy(
        scale_recv.at[pl.ds(0, EV - 1)], scale_recv.at[pl.ds(0, EV - 1)], scale_sem.at[0]
    ).wait()
    pltpu.make_async_copy(
        part_recv.at[pl.ds(0, EV - 1)], part_recv.at[pl.ds(0, EV - 1)], part_sem.at[0]
    ).wait()
    for step in range(4):
        for way in range(2):
            ring_copy(way, step).wait_send()
    for order in range(8):
        pair_copy(order).wait_send()


def shards(
    sink_elemental,
    source_elemental,
    perambulator,
    diagram_time,
    diagram_perm,
    diagram_ops,
    diagram_sign,
):
    source = jnp.transpose(source_elemental, (0, 1, 3, 4, 2)).reshape(2, NS, ROWS, NEV)
    count = diagram_time.shape[0]
    whole = pl.BlockSpec(memory_space=pl.ANY)
    near = pl.BlockSpec(memory_space=pltpu.VMEM)
    dma = pltpu.SemaphoreType.DMA
    blocks, correlator = pl.pallas_call(
        kernel,
        out_shape=(
            jax.ShapeDtypeStruct((2, NEV), F32),
            jax.ShapeDtypeStruct((2, NEV), F32),
        ),
        in_specs=[whole, whole, near, near, near, near, near],
        out_specs=(near, near),
        scratch_shapes=[
            pltpu.VMEM((BLOCK, 2, NS, NEV, NEV), BF16),
            pltpu.VMEM((EV, BLOCK, ROWS, NEV), jnp.int32),
            pltpu.VMEM((BLOCK, EV, ROWS, NEV), jnp.int32),
            pltpu.VMEM((TM, 2, NS, ROWS, NEV), BF16),
            pltpu.VMEM((BLOCK, 512, EV * NEV), BF16),
            pltpu.VMEM((2 * BLOCK * 2 * NEV, NEV), F32),
            pltpu.VMEM((256, EV * NEV), BF16),
            pltpu.VMEM((512, 256), F32),
            pltpu.VMEM((NS, NEV), F32),
            pltpu.VMEM((EV, NS, NEV), F32),
            pltpu.VMEM((BLOCK, EV, NS, NEV), F32),
            pltpu.VMEM((256, 256), BF16),
            pltpu.VMEM((512, 256), BF16),
            pltpu.VMEM((256, 256), BF16),
            pltpu.VMEM((NEV, NEV), F32),
            pltpu.VMEM((2, NEV), F32),
            pltpu.VMEM((EV, 2, NEV), F32),
            dma((BLOCK,)),
            dma((BLOCK,)),
            dma((BLOCK,)),
            dma((BLOCK,)),
            dma((2,)),
            dma((2,)),
            dma((2, 2, 4)),
            dma((2, 8)),
            dma,
        ],
        compiler_params=pltpu.CompilerParams(
            collective_id=0, has_side_effects=True, vmem_limit_bytes=60 << 20
        ),
        cost_estimate=pl.CostEstimate(
            flops=17 * 10**9, bytes_accessed=5 << 20, transcendentals=0
        ),
    )(
        sink_elemental,
        source,
        perambulator,
        diagram_time.reshape(1, count),
        diagram_perm.T,
        diagram_ops.T,
        diagram_sign.reshape(1, count),
    )
    return blocks.reshape(2, 1, 2, NS, NS), correlator[:, :1]


def solution(mesh):
    placed = (
        P(None, "tm", None, "evec", None, None),
        P(None, None, None, "evec", "tm"),
        P(None, "tm", None, None),
        P(),
        P(),
        P(),
        P(),
    )
    return jax.shard_map(
        shards,
        mesh=mesh,
        in_specs=placed,
        out_specs=(P(None, "tm", None, None, None), P(None, "tm")),
        check_vma=False,
    )
```

profile of v0, /device:TPU:1, one launch (start us, length us, event | category | flops | bytes accessed | tf_op | source)
XLA Modules:
  0.0 77.2 jit_solution(8707703929882513225)
XLA Ops:
  0.6 73.9 %shard_map.86 = (f32[2,128]{1,0:T(2,128)}, f32[2,128]{1,0:T(2,128)}) custom-call(bf16[2,1,8,8,128,128]{5,4,3,2,1,0:T(8,128)(2,1)} %sink_ref.1, bf16[2,8,64,128]{3,2,1,0:T(8,128)(2,1)} %bitcast.10, bf16[2,1,128,128]{3,2,1,0:T(8,128)(2,1)} %peram_ref.1, s32[1,1024]{1,0:T(1,128)} %bitcast.13, s32[2,1024]{1,0:T(2,128)} %bitcast.12, s32[4,1024]{1,0:T(4,128)} %bitcast.11, ...), custom_call_target="tpu_custom_call" | custom-call | flops 16999999488 | bytes 5242880 | tf_op jit(solution)/shard_map/pallas_call | solution.py:402
  74.6 1.2 %copy.10 = f32[2,1]{0,1:T(1,128)} copy(f32[2,1]{1,0:T(2,128)} %bitcast.15) | data formatting | bytes 16
  75.8 1.4 %reshape.19 = f32[2,1,2,8,8]{4,3,2,0,1:T(8,128)} reshape(f32[2,128]{1,0:T(2,128)} %get-tuple-element.4) | data formatting | bytes 2048 | tf_op jit(solution)/shard_map/reshape | solution.py:453
where the time goes:
time: 77.5 us; the launch traced here: 77.2 us
  Pallas kernels  73.9 us (95%)
  local copies, waits for them, and re-layouts  2.6 us (3%)
    pallas_call x1, Pallas kernels, shards(): pl.pallas_call(kernel, out_shape=(jax.ShapeDtypeStruct((2, NEV), F32), ja...  73.9 us

commit v1 on v0

v1 whole, which is shorter than its diff:
```python
import functools
import math

import jax
import jax.numpy as jnp
from jax import lax
from jax.experimental import pallas as pl
from jax.experimental.pallas import tpu as pltpu
from jax.sharding import PartitionSpec as P

DIAG_T = 64
NEV = 128
NS = 8
BLOCK = 8
EV = 16
TM = 16
ZS = 8
ROWS = NS * BLOCK
RINGS = 7
TOP = 32767.0
MESH = pl.DeviceIdType.MESH
F32 = jnp.float32
BF16 = jnp.bfloat16
NT = (((1,), (1,)), ((), ()))
NN = (((1,), (0,)), ((), ()))
FAR_FIRST = (10, 9, 11, 6, 14, 2, 8, 5, 7, 13, 15, 1, 3, 4, 12)


def split_parts(value):
    high = value.astype(BF16)
    return high, (value - high.astype(F32)).astype(BF16)


def iota(shape, axis):
    return lax.broadcasted_iota(jnp.int32, shape, axis)


def kernel(
    sink_ref,
    source_ref,
    peram_ref,
    time_ref,
    perm_ref,
    ops_ref,
    sign_ref,
    blocks_ref,
    corr_ref,
    sink_buf,
    send,
    recv,
    gathered,
    rmat,
    stage,
    tmat,
    total,
    scale_own,
    scale_recv,
    wide,
    left_mat,
    right_mat,
    source_mat,
    counts,
    spread,
    part_own,
    part_recv,
    sink_sem,
    send_sem,
    recv_sem,
    own_sem,
    scale_sem,
    part_sem,
    ring_sem,
    pair_sem,
    first_sem,
    slot_sem,
):
    tm = lax.axis_index("tm")
    ev = lax.axis_index("evec")
    row, column = ev // 4, lax.rem(ev, 4)
    depth, core = tm // 2, lax.rem(tm, 2)

    def peer(step):
        return lax.rem(row + step // 4, 4) * 4 + lax.rem(column + step % 4, 4)

    def slot(step):
        return lax.rem(depth + step + ZS, ZS) * 2 + core

    up, down = (slot(1), ev), (slot(-1), ev)
    pair = (depth * 2 + 1 - core, ev)

    def sink_copy(a):
        return pltpu.make_async_copy(
            sink_ref.at[:, 0, :, a], sink_buf.at[a], sink_sem.at[a]
        )

    for a in range(BLOCK):
        sink_copy(a).start()

    barrier = pltpu.get_barrier_semaphore()
    for step in FAR_FIRST:
        pl.semaphore_signal(barrier, inc=1, device_id=(tm, peer(step)), device_id_type=MESH)
    for device in (up, down, pair):
        pl.semaphore_signal(barrier, inc=1, device_id=device, device_id_type=MESH)

    real, imag = peram_ref[0, 0], peram_ref[1, 0]
    real32, imag32 = real.astype(F32), imag.astype(F32)
    real_t, imag_t = real32.T.astype(BF16), imag32.T.astype(BF16)
    minus, minus_t = (-imag32).astype(BF16), (-imag32.T).astype(BF16)
    left_mat[...] = jnp.concatenate(
        [jnp.concatenate([real_t, minus_t], 1), jnp.concatenate([imag_t, real_t], 1)], 0
    )
    one = jnp.concatenate(
        [jnp.concatenate([real, imag], 1), jnp.concatenate([minus, real], 1)], 0
    )
    right_mat[...] = jnp.concatenate([one, one], 0)
    source_mat[...] = jnp.concatenate(
        [jnp.concatenate([real, minus], 1), jnp.concatenate([imag, real], 1)], 0
    )

    def transform(a):
        for s2 in range(NS // 2):
            s = 2 * s2
            both = jnp.concatenate(
                [
                    jnp.concatenate([sink_buf[a, 0, s], sink_buf[a, 0, s + 1]], 1),
                    jnp.concatenate([sink_buf[a, 1, s], sink_buf[a, 1, s + 1]], 1),
                ],
                0,
            )
            once = lax.dot_general(left_mat[...], both, NN, preferred_element_type=F32)
            high, low = split_parts(once)
            lines = []
            for h in range(2):
                lanes = slice(h * NEV, (h + 1) * NEV)
                lines.append(
                    jnp.concatenate(
                        [high[:NEV, lanes], high[NEV:, lanes], low[:NEV, lanes], low[NEV:, lanes]], 1
                    )
                )
            wide[pl.ds(s * NEV, 2 * NEV), :] = lax.dot_general(
                jnp.concatenate(lines, 0), right_mat[...], NN, preferred_element_type=F32
            )
        for there in range(EV):
            value = jnp.concatenate(
                [wide[pl.ds(s * NEV + there * BLOCK, BLOCK), :] for s in range(NS)], 0
            )
            top = jnp.max(jnp.abs(value), axis=0, keepdims=True)
            top = jnp.maximum(jnp.maximum(top[:, :NEV], top[:, NEV:]), 1e-35)
            factor = TOP / top
            real_code = jnp.round(value[:, :NEV] * factor).astype(jnp.int32)
            imag_code = jnp.round(value[:, NEV:] * factor).astype(jnp.int32)
            send[there, a] = (real_code << 16) | (imag_code & 0xFFFF)
            scale_own[there, a] = top * (1.0 / TOP)

    def send_copy(a, step):
        there = peer(step)
        return pltpu.make_async_remote_copy(
            send.at[there, a], recv.at[a, ev], send_sem.at[a], recv_sem.at[a],
            device_id=(tm, there), device_id_type=MESH,
        )

    def scale_copy(a, step):
        there = peer(step)
        return pltpu.make_async_remote_copy(
            scale_own.at[there, a], scale_recv.at[a, ev], scale_sem.at[0, a], scale_sem.at[1, a],
            device_id=(tm, there), device_id_type=MESH,
        )

    def own_copy(a):
        return pltpu.make_async_copy(send.at[ev, a], recv.at[a, ev], own_sem.at[a])

    def post(a):
        for step in FAR_FIRST:
            scale_copy(a, step).start()
            send_copy(a, step).start()
        own_copy(a).start()
        scale_recv[a, ev] = scale_own[ev, a]

    def arrived(ref, sem):
        pltpu.make_async_copy(ref, ref, sem).wait()

    def ring_copy(way, message):
        step, half = message // 2, lax.rem(message + way, 2)
        index = slot(step * (2 * way - 1))
        src = source_ref.at[half] if isinstance(message, int) else gathered.at[index, half]
        return pltpu.make_async_remote_copy(
            src, gathered.at[index, half], ring_sem.at[0, way, message],
            ring_sem.at[1, way, message], device_id=(up, down)[way], device_id_type=MESH,
        )

    def ring_arrival(way, message):
        index = slot((message // 2 + 1) * (2 * way - 1))
        return gathered.at[index, lax.rem(message + way, 2)]

    def pair_copy(way, message):
        ref = ring_arrival(way, message)
        return pltpu.make_async_remote_copy(
            ref, ref, pair_sem.at[0, way, message], pair_sem.at[1, way, message],
            device_id=pair, device_id_type=MESH,
        )

    def pair_arrival(way, message):
        index = slot((message // 2 + 1) * (2 * way - 1)) + 1 - 2 * core
        return gathered.at[index, lax.rem(message + way, 2)]

    pair_first = pltpu.make_async_remote_copy(
        source_ref, gathered.at[tm], first_sem.at[0], first_sem.at[1],
        device_id=pair, device_id_type=MESH,
    )
    own_source = pltpu.make_async_copy(source_ref, gathered.at[tm], slot_sem)

    def relay(message):
        for way in range(2):
            arrived(ring_arrival(way, message), ring_sem.at[1, way, message])
            pair_copy(way, message).start()

        @pl.when(message < 4)
        def _():
            for way in range(2):
                ring_copy(way, message + 2).start()

        @pl.when(message == 4)
        def _():
            ring_copy(0, message + 2).start()

        @pl.when(message == 5)
        def _():
            ring_copy(1, message + 1).start()

    own_source.start()
    pl.semaphore_wait(barrier, EV - 1 + 3)
    for message in range(2):
        for way in range(2):
            ring_copy(way, message).start()
    pair_first.start()
    sink_copy(0).wait()
    transform(0)
    post(0)

    @pl.loop(1, BLOCK)
    def _(a):
        sink_copy(a).wait()
        transform(a)
        post(a)
        relay(a - 1)

    def position(first):
        nucleon = first // 2
        return (
            perm_ref[nucleon : nucleon + 1, :] * NS + ops_ref[first : first + 1, :]
        ) * NS + ops_ref[first + 1 : first + 2, :]

    phase = jnp.where(time_ref[...] == tm, 1 - 2 * sign_ref[...], 0).astype(F32)
    entries = iota((NEV, phase.shape[1]), 0)
    first_hot = jnp.where(entries == position(0), phase, 0.0).astype(BF16)
    second_hot = jnp.where(entries == position(2), 1.0, 0.0).astype(BF16)
    counts[...] = lax.dot_general(first_hot, second_hot, NT, preferred_element_type=F32)

    own_source.wait()
    arrived(gathered.at[tm + 1 - 2 * core], first_sem.at[1])

    @pl.loop(0, RINGS)
    def _(message):
        for way in range(2):
            arrived(pair_arrival(way, message), pair_sem.at[1, way, message])

    @pl.loop(0, NS)
    def _(u):
        for j2 in range(BLOCK // 2):
            mats = []
            for part in range(2):
                lines = gathered[:, part, u, pl.ds(j2 * 2 * BLOCK, 2 * BLOCK), :].astype(F32)
                mats.append(
                    [
                        lines[:, h * BLOCK : (h + 1) * BLOCK].reshape(NEV, NEV).astype(BF16)
                        for h in range(2)
                    ]
                )
            by_rows = jnp.concatenate(
                [jnp.concatenate([mats[0][h], mats[1][h]], 1) for h in range(2)], 0
            )
            by_lanes = jnp.concatenate(
                [jnp.concatenate([mats[part][0], mats[part][1]], 1) for part in range(2)], 0
            )
            direct = lax.dot_general(source_mat[...], by_rows, NT, preferred_element_type=F32)
            crossed = lax.dot_general(source_mat[...], by_lanes, NN, preferred_element_type=F32)
            for p, result in enumerate((direct, crossed)):
                for h in range(2):
                    at = (p * BLOCK + 2 * j2 + h) * 2 * NEV
                    stage[pl.ds(at, 2 * NEV), :] = result[:, h * NEV : (h + 1) * NEV]

        @pl.loop(0, EV)
        def _(block):
            lanes = pl.ds(pl.multiple_of(block * NEV, NEV), NEV)
            for p in range(2):
                turned = []
                for part in range(2):
                    tiles = [
                        stage[
                            pl.ds((p * BLOCK + j) * 2 * NEV + part * NEV + block * BLOCK, BLOCK), :
                        ]
                        for j in range(BLOCK)
                    ]
                    turned.append(jnp.swapaxes(jnp.stack(tiles, 0), 0, 1))
                rows = pl.ds(pl.multiple_of((p * NS + u) * 32, 32), 32)
                for a in range(BLOCK):
                    parts = []
                    for part in range(2):
                        value = turned[part][a]
                        parts += [value, value - value.astype(BF16).astype(F32)]
                    rmat[a, rows, lanes] = jnp.concatenate(parts, 0).astype(BF16)

    total[...] = jnp.zeros_like(total)
    tile_row, entry = iota((256, 256), 0), iota((256, 256), 1)
    spread[...] = jnp.where(
        (tile_row // 128 == entry // 128) & (tile_row // BLOCK % NS == entry // NS % NS), 1.0, 0.0
    ).astype(BF16)

    others = pl.ds(0, EV - 1)

    @pl.loop(0, BLOCK)
    def _(a):
        own_copy(a).wait()
        arrived(scale_recv.at[a, others], scale_sem.at[1, a])
        arrived(recv.at[a, others], recv_sem.at[a])
        for block in range(EV):
            scale = scale_recv[a, block]
            packed = recv[a, block]
            real_high, real_low = split_parts((packed >> 16).astype(F32) * scale)
            imag_high, imag_low = split_parts(((packed << 16) >> 16).astype(F32) * scale)
            tmat[:, block * NEV : (block + 1) * NEV] = jnp.concatenate(
                [real_high, real_low, imag_high, imag_low], 0
            )
        total[...] += lax.dot_general(rmat[a], tmat[...], NT, preferred_element_type=F32)

    alike = (iota((512, 256), 0) % BLOCK) == (iota((512, 256), 1) % BLOCK)
    kept = jnp.where(alike, total[...], 0.0).reshape(32, 16, 256).sum(axis=1)
    high = kept.astype(BF16)
    rest = kept - high.astype(F32)
    middle, low = split_parts(rest)
    lined = lax.dot_general(
        jnp.concatenate([high, middle, low], 0), spread[...], NN, preferred_element_type=F32
    ).reshape(3, 32, 256)
    lined = lined[0] + (lined[1] + lined[2])
    line, entry = iota((32, 128), 0), iota((32, 128), 1)
    wanted = (line // 16 == entry // 64) & (line // 2 % NS == entry % NS)
    real_line = line % 2 == 0
    with_real, with_imag = lined[:, :NEV], lined[:, NEV:]
    real_sum = jnp.where(wanted, jnp.where(real_line, with_real, -with_imag), 0.0)
    imag_sum = jnp.where(wanted, jnp.where(real_line, with_imag, with_real), 0.0)
    part_own[...] = jnp.concatenate(
        [real_sum.sum(axis=0, keepdims=True), imag_sum.sum(axis=0, keepdims=True)], 0
    )

    def part_copy(step):
        return pltpu.make_async_remote_copy(
            part_own, part_recv.at[ev], part_sem.at[0], part_sem.at[1],
            device_id=(tm, peer(step)), device_id_type=MESH,
        )

    for step in FAR_FIRST:
        part_copy(step).start()
    part_recv[ev] = part_own[...]
    arrived(part_recv.at[others], part_sem.at[1])
    blocks = part_recv[0]
    for block in range(1, EV):
        blocks = blocks + part_recv[block]
    blocks = blocks * NEV ** (-1.5)
    line, entry = iota((32, NEV), 0), iota((32, NEV), 1)
    lines = jnp.concatenate(
        [jnp.broadcast_to(blocks[part : part + 1], (16, NEV)) for part in range(2)], 0
    )
    lines = jnp.where(line % 16 == entry // NS, lines, 0.0)
    picked = iota((NEV, NS), 0) % NS == iota((NEV, NS), 1)
    blocks_ref[...] = lax.dot_general(
        lines, jnp.where(picked, 1.0, 0.0), NN,
        precision=lax.Precision.HIGHEST, preferred_element_type=F32,
    ).reshape(blocks_ref.shape)
    met = lax.dot_general(
        blocks, counts[...], NN, precision=lax.Precision.HIGHEST, preferred_element_type=F32
    )
    real_value = met[0:1] * blocks[0:1] - met[1:2] * blocks[1:2]
    imag_value = met[0:1] * blocks[1:2] + met[1:2] * blocks[0:1]
    value = [part.sum(axis=1, keepdims=True) for part in (real_value, imag_value)]
    corr_ref[...] = jnp.concatenate(value, 1) / math.sqrt(DIAG_T)

    @pl.loop(0, BLOCK)
    def _(a):
        arrived(recv.at[a, others], send_sem.at[a])
        arrived(scale_recv.at[a, others], scale_sem.at[0, a])

    arrived(part_recv.at[others], part_sem.at[0])
    pair_first.wait_send()

    @pl.loop(0, RINGS)
    def _(message):
        for way in range(2):
            arrived(pair_arrival(way, message), ring_sem.at[0, way, message])
            arrived(pair_arrival(way, message), pair_sem.at[0, way, message])


def place(blocks_in, corr_in, blocks_ref, corr_ref):
    blocks_ref[...] = blocks_in[...]
    corr_ref[...] = corr_in[...]


def shards(
    sink_elemental,
    source_elemental,
    perambulator,
    diagram_time,
    diagram_perm,
    diagram_ops,
    diagram_sign,
):
    source = jnp.transpose(source_elemental, (0, 1, 3, 4, 2)).reshape(2, NS, ROWS, NEV)
    count = diagram_time.shape[0]
    whole = pl.BlockSpec(memory_space=pl.ANY)
    near = pl.BlockSpec(memory_space=pltpu.VMEM)
    dma = pltpu.SemaphoreType.DMA
    blocks, correlator = pl.pallas_call(
        kernel,
        out_shape=(
            jax.ShapeDtypeStruct((2, 1, 2, NS, NS), F32),
            jax.ShapeDtypeStruct((1, 2), F32),
        ),
        in_specs=[whole, whole, near, near, near, near, near],
        out_specs=(near, near),
        scratch_shapes=[
            pltpu.VMEM((BLOCK, 2, NS, NEV, NEV), BF16),
            pltpu.VMEM((EV, BLOCK, ROWS, NEV), jnp.int32),
            pltpu.VMEM((BLOCK, EV, ROWS, NEV), jnp.int32),
            pltpu.VMEM((TM, 2, NS, ROWS, NEV), BF16),
            pltpu.VMEM((BLOCK, 512, EV * NEV), BF16),
            pltpu.VMEM((2 * BLOCK * 2 * NEV, NEV), F32),
            pltpu.VMEM((256, EV * NEV), BF16),
            pltpu.VMEM((512, 256), F32),
            pltpu.VMEM((EV, BLOCK, 1, NEV), F32),
            pltpu.VMEM((BLOCK, EV, 1, NEV), F32),
            pltpu.VMEM((NS * NEV, 2 * NEV), F32),
            pltpu.VMEM((256, 256), BF16),
            pltpu.VMEM((512, 256), BF16),
            pltpu.VMEM((256, 256), BF16),
            pltpu.VMEM((NEV, NEV), F32),
            pltpu.VMEM((256, 256), BF16),
            pltpu.VMEM((2, NEV), F32),
            pltpu.VMEM((EV, 2, NEV), F32),
            dma((BLOCK,)),
            dma((BLOCK,)),
            dma((BLOCK,)),
            dma((BLOCK,)),
            dma((2, BLOCK)),
            dma((2,)),
            dma((2, 2, RINGS)),
            dma((2, 2, RINGS)),
            dma((2,)),
            dma,
        ],
        compiler_params=pltpu.CompilerParams(
            collective_id=0, has_side_effects=True, vmem_limit_bytes=60 << 20
        ),
        cost_estimate=pl.CostEstimate(
            flops=17 * 10**9, bytes_accessed=5 << 20, transcendentals=0
        ),
    )(
        sink_elemental,
        source,
        perambulator,
        diagram_time.reshape(1, count),
        diagram_perm.T,
        diagram_ops.T,
        diagram_sign.reshape(1, count),
    )
    blocks, correlator = pl.pallas_call(
        place,
        out_shape=(
            jax.ShapeDtypeStruct(blocks.shape, F32),
            jax.ShapeDtypeStruct(correlator.shape, F32),
        ),
        in_specs=[near, near],
        out_specs=(near, near),
    )(blocks, correlator)
    return blocks, correlator.T


def solution(mesh):
    placed = (
        P(None, "tm", None, "evec", None, None),
        P(None, None, None, "evec", "tm"),
        P(None, "tm", None, None),
        P(),
        P(),
        P(),
        P(),
    )
    return jax.shard_map(
        shards,
        mesh=mesh,
        in_specs=placed,
        out_specs=(P(None, "tm", None, None, None), P(None, "tm")),
        check_vma=False,
    )
```

time: 77.5 us -> 67.5 us (0.87)
  Pallas kernels: 73.9 us -> 66.6 us
  local copies, waits for them, and re-layouts: 2.6 us -> 0 us
    pallas_call x1 -> x2, Pallas kernels: 73.9 us -> 66.6 us  [the longest x1 65.3 us: shards(): pl.pallas_call(kernel, out_shape=(jax.ShapeDtypeStruct((2, 1, 2, NS, NS),...]
    reshape x1 -> x0, local copies, waits for them, and re-layouts: 1.35 us -> none  [shards(): return (blocks.reshape(2, 1, 2, NS, NS), correlator[:, :1])]
    unnamed x1 -> x0, local copies, waits for them, and re-layouts: 1.24 us -> none
where the time goes in v1:
time: 67.5 us; the launch traced here: 67.3 us
  Pallas kernels  66.6 us (99%)
    pallas_call x1, Pallas kernels, shards(): pl.pallas_call(kernel, out_shape=(jax.ShapeDtypeStruct((2, 1, 2, NS, NS),...  65.3 us

profile of v1, /device:TPU:1, one launch (start us, length us, event | category | flops | bytes accessed | tf_op | source)
XLA Modules:
  0.0 67.3 jit_solution(4329003266347752903)
XLA Ops:
  0.6 65.3 %shard_map.86 = (f32[2,1,2,8,8]{4,3,2,1,0:T(8,128)}, f32[1,2]{1,0:T(1,128)}) custom-call(bf16[2,1,8,8,128,128]{5,4,3,2,1,0:T(8,128)(2,1)} %sink_ref.1, bf16[2,8,64,128]{3,2,1,0:T(8,128)(2,1)} %bitcast.8, bf16[2,1,128,128]{3,2,1,0:T(8,128)(2,1)} %peram_ref.1, s32[1,1024]{1,0:T(1,128)} %bitcast.11, s32[2,1024]{1,0:T(2,128)} %bitcast.10, s32[4,1024]{1,0:T(4,128)} %bitcast.9, ...), custom_call_target="tpu_custom_call" | custom-call | flops 16999999488 | bytes 5242880 | tf_op jit(solution)/shard_map/pallas_call | solution.py:421
  66.0 1.3 %shard_map.87 = (f32[2,1,2,8,8]{4,3,2,1,0:T(8,128)}, f32[1,2]{1,0:T(1,128)}) custom-call(f32[2,1,2,8,8]{4,3,2,1,0:T(8,128)} %get-tuple-element.6.blocks_in, f32[1,2]{1,0:T(1,128)} %get-tuple-element.7.corr_in), custom_call_target="tpu_custom_call" | custom-call | tf_op jit(solution)/shard_map/pallas_call | solution.py:474

commit v2 on v1

--- a/solution.py
+++ b/solution.py
@@ -31,6 +31,12 @@
     return high, (value - high.astype(F32)).astype(BF16)
 
 
+def three_parts(value):
+    high = value.astype(BF16)
+    middle, low = split_parts(value - high.astype(F32))
+    return jnp.concatenate([high, middle, low], 0)
+
+
 def iota(shape, axis):
     return lax.broadcasted_iota(jnp.int32, shape, axis)
 
@@ -38,13 +44,18 @@
 def kernel(
     sink_ref,
     source_ref,
+    peram_in,
+    time_in,
+    perm_in,
+    ops_in,
+    sign_in,
+    blocks_ref,
+    corr_ref,
     peram_ref,
     time_ref,
     perm_ref,
     ops_ref,
     sign_ref,
-    blocks_ref,
-    corr_ref,
     sink_buf,
     send,
     recv,
@@ -73,6 +84,7 @@
     pair_sem,
     first_sem,
     slot_sem,
+    small_sem,
 ):
     tm = lax.axis_index("tm")
     ev = lax.axis_index("evec")
@@ -93,14 +105,28 @@
             sink_ref.at[:, 0, :, a], sink_buf.at[a], sink_sem.at[a]
         )
 
-    for a in range(BLOCK):
-        sink_copy(a).start()
-
+    small = [
+        pltpu.make_async_copy(whole, near, small_sem.at[at])
+        for at, (whole, near) in enumerate(
+            (
+                (peram_in, peram_ref),
+                (time_in, time_ref),
+                (perm_in, perm_ref),
+                (ops_in, ops_ref),
+                (sign_in, sign_ref),
+            )
+        )
+    ]
+    small[0].start()
+    sink_copy(0).start()
     barrier = pltpu.get_barrier_semaphore()
     for step in FAR_FIRST:
         pl.semaphore_signal(barrier, inc=1, device_id=(tm, peer(step)), device_id_type=MESH)
     for device in (up, down, pair):
         pl.semaphore_signal(barrier, inc=1, device_id=device, device_id_type=MESH)
+    for a in range(1, BLOCK):
+        sink_copy(a).start()
+    small[0].wait()
 
     real, imag = peram_ref[0, 0], peram_ref[1, 0]
     real32, imag32 = real.astype(F32), imag.astype(F32)
@@ -140,17 +166,21 @@
             wide[pl.ds(s * NEV, 2 * NEV), :] = lax.dot_general(
                 jnp.concatenate(lines, 0), right_mat[...], NN, preferred_element_type=F32
             )
-        for there in range(EV):
-            value = jnp.concatenate(
-                [wide[pl.ds(s * NEV + there * BLOCK, BLOCK), :] for s in range(NS)], 0
-            )
-            top = jnp.max(jnp.abs(value), axis=0, keepdims=True)
-            top = jnp.maximum(jnp.maximum(top[:, :NEV], top[:, NEV:]), 1e-35)
-            factor = TOP / top
-            real_code = jnp.round(value[:, :NEV] * factor).astype(jnp.int32)
-            imag_code = jnp.round(value[:, NEV:] * factor).astype(jnp.int32)
-            send[there, a] = (real_code << 16) | (imag_code & 0xFFFF)
-            scale_own[there, a] = top * (1.0 / TOP)
+    def encode(a, there):
+        value = jnp.concatenate(
+            [
+                wide[pl.ds(pl.multiple_of(s * NEV + there * BLOCK, BLOCK), BLOCK), :]
+                for s in range(NS)
+            ],
+            0,
+        )
+        top = jnp.max(jnp.abs(value), axis=0, keepdims=True)
+        top = jnp.maximum(jnp.maximum(top[:, :NEV], top[:, NEV:]), 1e-35)
+        factor = TOP / top
+        real_code = jnp.round(value[:, :NEV] * factor).astype(jnp.int32)
+        imag_code = jnp.round(value[:, NEV:] * factor).astype(jnp.int32)
+        send[there, a] = (real_code << 16) | (imag_code & 0xFFFF)
+        scale_own[there, a] = top * (1.0 / TOP)
 
     def send_copy(a, step):
         there = peer(step)
@@ -171,8 +201,10 @@
 
     def post(a):
         for step in FAR_FIRST:
+            encode(a, peer(step))
             scale_copy(a, step).start()
             send_copy(a, step).start()
+        encode(a, ev)
         own_copy(a).start()
         scale_recv[a, ev] = scale_own[ev, a]
 
@@ -227,15 +259,18 @@
         def _():
             ring_copy(1, message + 1).start()
 
-    own_source.start()
     pl.semaphore_wait(barrier, EV - 1 + 3)
     for message in range(2):
         for way in range(2):
             ring_copy(way, message).start()
     pair_first.start()
+    own_source.start()
     sink_copy(0).wait()
     transform(0)
     post(0)
+
+    for copy in small[1:]:
+        copy.start()
 
     @pl.loop(1, BLOCK)
     def _(a):
@@ -250,11 +285,18 @@
             perm_ref[nucleon : nucleon + 1, :] * NS + ops_ref[first : first + 1, :]
         ) * NS + ops_ref[first + 1 : first + 2, :]
 
+    for copy in small[1:]:
+        copy.wait()
     phase = jnp.where(time_ref[...] == tm, 1 - 2 * sign_ref[...], 0).astype(F32)
     entries = iota((NEV, phase.shape[1]), 0)
     first_hot = jnp.where(entries == position(0), phase, 0.0).astype(BF16)
     second_hot = jnp.where(entries == position(2), 1.0, 0.0).astype(BF16)
-    counts[...] = lax.dot_general(first_hot, second_hot, NT, preferred_element_type=F32)
+    counts[...] = jnp.concatenate(
+        split_parts(
+            lax.dot_general(first_hot, second_hot, NT, preferred_element_type=F32)
+        ),
+        1,
+    )
 
     own_source.wait()
     arrived(gathered.at[tm + 1 - 2 * core], first_sem.at[1])
@@ -317,10 +359,19 @@
     ).astype(BF16)
 
     others = pl.ds(0, EV - 1)
+    pair_first.wait_send()
+
+    @pl.loop(0, RINGS)
+    def _(message):
+        for way in range(2):
+            arrived(pair_arrival(way, message), ring_sem.at[0, way, message])
+            arrived(pair_arrival(way, message), pair_sem.at[0, way, message])
 
     @pl.loop(0, BLOCK)
     def _(a):
         own_copy(a).wait()
+        arrived(scale_recv.at[a, others], scale_sem.at[0, a])
+        arrived(recv.at[a, others], send_sem.at[a])
         arrived(scale_recv.at[a, others], scale_sem.at[1, a])
         arrived(recv.at[a, others], recv_sem.at[a])
         for block in range(EV):
@@ -335,11 +386,8 @@
 
     alike = (iota((512, 256), 0) % BLOCK) == (iota((512, 256), 1) % BLOCK)
     kept = jnp.where(alike, total[...], 0.0).reshape(32, 16, 256).sum(axis=1)
-    high = kept.astype(BF16)
-    rest = kept - high.astype(F32)
-    middle, low = split_parts(rest)
     lined = lax.dot_general(
-        jnp.concatenate([high, middle, low], 0), spread[...], NN, preferred_element_type=F32
+        three_parts(kept), spread[...], NN, preferred_element_type=F32
     ).reshape(3, 32, 256)
     lined = lined[0] + (lined[1] + lined[2])
     line, entry = iota((32, 128), 0), iota((32, 128), 1)
@@ -372,31 +420,23 @@
     )
     lines = jnp.where(line % 16 == entry // NS, lines, 0.0)
     picked = iota((NEV, NS), 0) % NS == iota((NEV, NS), 1)
-    blocks_ref[...] = lax.dot_general(
-        lines, jnp.where(picked, 1.0, 0.0), NN,
-        precision=lax.Precision.HIGHEST, preferred_element_type=F32,
-    ).reshape(blocks_ref.shape)
+    final = lax.dot_general(
+        three_parts(lines), jnp.where(picked, 1.0, 0.0).astype(BF16), NN,
+        preferred_element_type=F32,
+    ).reshape(3, 32, NS)
+    blocks_ref[...] = (final[0] + (final[1] + final[2])).reshape(blocks_ref.shape)
+    padded = jnp.concatenate([blocks, jnp.zeros((14, NEV), F32)], 0)
     met = lax.dot_general(
-        blocks, counts[...], NN, precision=lax.Precision.HIGHEST, preferred_element_type=F32
-    )
+        three_parts(padded), counts[...], NN, preferred_element_type=F32
+    ).reshape(3, 16, 2 * NEV)
+    met = met[0] + (met[1] + met[2])
+    met = met[:, :NEV] + met[:, NEV:]
     real_value = met[0:1] * blocks[0:1] - met[1:2] * blocks[1:2]
     imag_value = met[0:1] * blocks[1:2] + met[1:2] * blocks[0:1]
     value = [part.sum(axis=1, keepdims=True) for part in (real_value, imag_value)]
     corr_ref[...] = jnp.concatenate(value, 1) / math.sqrt(DIAG_T)
 
-    @pl.loop(0, BLOCK)
-    def _(a):
-        arrived(recv.at[a, others], send_sem.at[a])
-        arrived(scale_recv.at[a, others], scale_sem.at[0, a])
-
     arrived(part_recv.at[others], part_sem.at[0])
-    pair_first.wait_send()
-
-    @pl.loop(0, RINGS)
-    def _(message):
-        for way in range(2):
-            arrived(pair_arrival(way, message), ring_sem.at[0, way, message])
-            arrived(pair_arrival(way, message), pair_sem.at[0, way, message])
 
 
 def place(blocks_in, corr_in, blocks_ref, corr_ref):
@@ -424,9 +464,14 @@
             jax.ShapeDtypeStruct((2, 1, 2, NS, NS), F32),
             jax.ShapeDtypeStruct((1, 2), F32),
         ),
-        in_specs=[whole, whole, near, near, near, near, near],
+        in_specs=[whole] * 7,
         out_specs=(near, near),
         scratch_shapes=[
+            pltpu.VMEM(perambulator.shape, BF16),
+            pltpu.VMEM((1, count), jnp.int32),
+            pltpu.VMEM((2, count), jnp.int32),
+            pltpu.VMEM((4, count), jnp.int32),
+            pltpu.VMEM((1, count), jnp.int32),
             pltpu.VMEM((BLOCK, 2, NS, NEV, NEV), BF16),
             pltpu.VMEM((EV, BLOCK, ROWS, NEV), jnp.int32),
             pltpu.VMEM((BLOCK, EV, ROWS, NEV), jnp.int32),
@@ -441,7 +486,7 @@
             pltpu.VMEM((256, 256), BF16),
             pltpu.VMEM((512, 256), BF16),
             pltpu.VMEM((256, 256), BF16),
-            pltpu.VMEM((NEV, NEV), F32),
+            pltpu.VMEM((NEV, 2 * NEV), BF16),
             pltpu.VMEM((256, 256), BF16),
             pltpu.VMEM((2, NEV), F32),
             pltpu.VMEM((EV, 2, NEV), F32),
@@ -455,6 +500,7 @@
             dma((2, 2, RINGS)),
             dma((2,)),
             dma,
+            dma((5,)),
         ],
         compiler_params=pltpu.CompilerParams(
             collective_id=0, has_side_effects=True, vmem_limit_bytes=60 << 20

time: 67.5 us -> 66.4 us (0.984)
  Pallas kernels: 66.6 us -> 65.6 us
    pallas_call x1, Pallas kernels: 65.3 us -> 64.3 us  [shards(): pl.pallas_call(kernel, out_shape=(jax.ShapeDtypeStruct((2, 1, 2, NS, NS),...]
where the time goes in v2:
time: 66.4 us; the launch traced here: 66.2 us
  Pallas kernels  65.6 us (99%)
    pallas_call x1, Pallas kernels, shards(): pl.pallas_call(kernel, out_shape=(jax.ShapeDtypeStruct((2, 1, 2, NS, NS),...  64.3 us
    pallas_call x1, Pallas kernels, shards(): pl.pallas_call(place, out_shape=(jax.ShapeDtypeStruct(blocks.shape, F32),...  1.33 us

profile of v2, /device:TPU:1, one launch (start us, length us, event | category | flops | bytes accessed | tf_op | source)
XLA Modules:
  0.0 66.2 jit_solution(639389262629607025)
XLA Ops:
  0.6 64.3 %shard_map.86 = (f32[2,1,2,8,8]{4,3,2,1,0:T(8,128)}, f32[1,2]{1,0:T(1,128)}) custom-call(bf16[2,1,8,8,128,128]{5,4,3,2,1,0:T(8,128)(2,1)} %sink_ref.1, bf16[2,8,64,128]{3,2,1,0:T(8,128)(2,1)} %bitcast.8, bf16[2,1,128,128]{3,2,1,0:T(8,128)(2,1)} %peram_in.1, s32[1,1024]{1,0:T(1,128)} %bitcast.11, s32[2,1024]{1,0:T(2,128)} %bitcast.10, s32[4,1024]{1,0:T(4,128)} %bitcast.9, ...), custom_call_target="tpu_custom_call" | custom-call | flops 16999999488 | bytes 5242880 | tf_op jit(solution)/shard_map/pallas_call | solution.py:461
  64.9 1.3 %shard_map.87 = (f32[2,1,2,8,8]{4,3,2,1,0:T(8,128)}, f32[1,2]{1,0:T(1,128)}) custom-call(f32[2,1,2,8,8]{4,3,2,1,0:T(8,128)} %get-tuple-element.6.blocks_in, f32[1,2]{1,0:T(1,128)} %get-tuple-element.7.corr_in), custom_call_target="tpu_custom_call" | custom-call | tf_op jit(solution)/shard_map/pallas_call | solution.py:520

commit v3 on v2

--- a/solution.py
+++ b/solution.py
@@ -259,14 +259,14 @@
         def _():
             ring_copy(1, message + 1).start()
 
+    sink_copy(0).wait()
+    transform(0)
     pl.semaphore_wait(barrier, EV - 1 + 3)
     for message in range(2):
         for way in range(2):
             ring_copy(way, message).start()
     pair_first.start()
     own_source.start()
-    sink_copy(0).wait()
-    transform(0)
     post(0)
 
     for copy in small[1:]:

time: 66.4 us -> 65.6 us (0.988)
  Pallas kernels: 65.6 us -> 64.8 us
    pallas_call x1, Pallas kernels: 64.3 us -> 63.5 us  [shards(): pl.pallas_call(kernel, out_shape=(jax.ShapeDtypeStruct((2, 1, 2, NS, NS),...]
where the time goes in v3:
time: 65.6 us; the launch traced here: 65.5 us
  Pallas kernels  64.8 us (99%)
    pallas_call x1, Pallas kernels, shards(): pl.pallas_call(kernel, out_shape=(jax.ShapeDtypeStruct((2, 1, 2, NS, NS),...  63.5 us
    pallas_call x1, Pallas kernels, shards(): pl.pallas_call(place, out_shape=(jax.ShapeDtypeStruct(blocks.shape, F32),...  1.33 us

profile of v3, /device:TPU:1, one launch (start us, length us, event | category | flops | bytes accessed | tf_op | source)
XLA Modules:
  0.0 65.5 jit_solution(13505359192337954604)
XLA Ops:
  0.6 63.5 %shard_map.86 = (f32[2,1,2,8,8]{4,3,2,1,0:T(8,128)}, f32[1,2]{1,0:T(1,128)}) custom-call(bf16[2,1,8,8,128,128]{5,4,3,2,1,0:T(8,128)(2,1)} %sink_ref.1, bf16[2,8,64,128]{3,2,1,0:T(8,128)(2,1)} %bitcast.8, bf16[2,1,128,128]{3,2,1,0:T(8,128)(2,1)} %peram_in.1, s32[1,1024]{1,0:T(1,128)} %bitcast.11, s32[2,1024]{1,0:T(2,128)} %bitcast.10, s32[4,1024]{1,0:T(4,128)} %bitcast.9, ...), custom_call_target="tpu_custom_call" | custom-call | flops 16999999488 | bytes 5242880 | tf_op jit(solution)/shard_map/pallas_call | solution.py:461
  64.1 1.3 %shard_map.87 = (f32[2,1,2,8,8]{4,3,2,1,0:T(8,128)}, f32[1,2]{1,0:T(1,128)}) custom-call(f32[2,1,2,8,8]{4,3,2,1,0:T(8,128)} %get-tuple-element.6.blocks_in, f32[1,2]{1,0:T(1,128)} %get-tuple-element.7.corr_in), custom_call_target="tpu_custom_call" | custom-call | tf_op jit(solution)/shard_map/pallas_call | solution.py:520

commit v4 on v3

--- a/solution.py
+++ b/solution.py
@@ -439,11 +439,6 @@
     arrived(part_recv.at[others], part_sem.at[0])
 
 
-def place(blocks_in, corr_in, blocks_ref, corr_ref):
-    blocks_ref[...] = blocks_in[...]
-    corr_ref[...] = corr_in[...]
-
-
 def shards(
     sink_elemental,
     source_elemental,
@@ -461,8 +456,8 @@
     blocks, correlator = pl.pallas_call(
         kernel,
         out_shape=(
-            jax.ShapeDtypeStruct((2, 1, 2, NS, NS), F32),
-            jax.ShapeDtypeStruct((1, 2), F32),
+            pltpu.VMEM((2, 1, 2, NS, NS), F32),
+            pltpu.VMEM((1, 2), F32),
         ),
         in_specs=[whole] * 7,
         out_specs=(near, near),
@@ -517,15 +512,6 @@
         diagram_ops.T,
         diagram_sign.reshape(1, count),
     )
-    blocks, correlator = pl.pallas_call(
-        place,
-        out_shape=(
-            jax.ShapeDtypeStruct(blocks.shape, F32),
-            jax.ShapeDtypeStruct(correlator.shape, F32),
-        ),
-        in_specs=[near, near],
-        out_specs=(near, near),
-    )(blocks, correlator)
     return blocks, correlator.T
 
 

time: 65.6 us -> 64.7 us (0.986)
  Pallas kernels: 64.8 us -> 62.9 us
  local copies, waits for them, and re-layouts: 0 us -> 1.12 us
    pallas_call x2 -> x1, Pallas kernels: 64.8 us -> 62.9 us  [shards(): pl.pallas_call(kernel, out_shape=(pltpu.VMEM((2, 1, 2, NS, NS), F32), plt...]
    unnamed x0 -> x2, local copies, waits for them, and re-layouts: none -> 1.12 us
where the time goes in v4:
time: 64.7 us; the launch traced here: 64.6 us
  Pallas kernels  62.9 us (97%)
  local copies, waits for them, and re-layouts  1.12 us (2%)
    pallas_call x1, Pallas kernels, shards(): pl.pallas_call(kernel, out_shape=(pltpu.VMEM((2, 1, 2, NS, NS), F32), plt...  62.9 us

profile of v4, /device:TPU:1, one launch (start us, length us, event | category | flops | bytes accessed | tf_op | source)
XLA Modules:
  0.0 64.6 jit_solution(7206163303386225556)
XLA Ops:
  0.6 62.9 %shard_map.86 = (f32[2,1,2,8,8]{4,3,2,1,0:T(8,128)S(1)}, f32[1,2]{1,0:T(1,128)S(1)}) custom-call(bf16[2,1,8,8,128,128]{5,4,3,2,1,0:T(8,128)(2,1)} %sink_ref.1, bf16[2,8,64,128]{3,2,1,0:T(8,128)(2,1)} %bitcast.9, bf16[2,1,128,128]{3,2,1,0:T(8,128)(2,1)} %peram_in.1, s32[1,1024]{1,0:T(1,128)} %bitcast.12, s32[2,1024]{1,0:T(2,128)} %bitcast.11, ...), custom_call_target="tpu_custom_call" | custom-call | flops 16999999488 | bytes 5242880 | tf_op jit(solution)/shard_map/pallas_call | solution.py:456
  63.5 0.6 copy.11
  64.1 0.5 copy.12
